TPU v7x, 256 devices: a whole 4x4x8 slice. The times are simulated.
256 devices in a mesh: row: 16 (over x, y), col: 16 (over z, core).
Axes of the slice: x: 4, y: 4, z: 8, core: 2. Of those that a mesh axis runs over, the one named last changes fastest.
Arguments:
- right_side: float32 [768, 32768], P('col', 'row'), may hold values from -6 to 6
- factor: float32 [32768, 2, 2048], P('row', None, 'col'), as said below
Outputs:
- result: float32 [768, 32768], P('col', 'row')
Inputs may be any that keep to these rules, and one draw needn't show every extreme that they name: factor[slab q, q, :] is lower-triangular with its diagonal between 0.5 and 1.5; factor[slab 0, 1, :] is zero; all other entries are the factor's off-diagonal blocks.
All inputs are finite; a program needn't handle non-finite values.
Results may differ from a plain program's by a relative error of at most 0.00011.
Values sent between devices are 32-bit elements; how exact they have to be, the bound alone decides.
A program may use at most 64 MiB of HBM per device.

v0:
```python
import jax
import jax.numpy as jnp
from jax import lax
from jax.sharding import PartitionSpec as P


def broadcast(value, axis, source):
    kept = jnp.where(lax.axis_index(axis) == source, value, 0).astype(value.dtype)
    return lax.psum(kept, axis)


def contract(left, right, left_dim, right_dim):
    return lax.dot_general(
        left,
        right,
        (((left_dim,), (right_dim,)), ((), ())),
        precision=lax.Precision.HIGHEST,
        preferred_element_type=jnp.float32,
    )


def local(right_side, factor):
    rhs_here = right_side.shape[0]
    row_place = lax.axis_index("row")
    current = right_side
    solved = []
    for panel in range(2):
        panel_block = factor[:, panel, :]
        spread = lax.all_to_all(current, "col", split_axis=1, concat_axis=0, tiled=True)

        def solve_term(offset, amount, source=spread, weights=panel_block):
            return contract(source, weights, 1, 1)

        local_solved = lax.psum_scatter(
            solve_term(jnp.int32(0), lax.axis_size("col") * rhs_here),
            "col",
            scatter_dimension=0,
            tiled=True,
        )
        solved_here = broadcast(local_solved, "row", panel)
        solved_spread = lax.all_to_all(solved_here, "col", split_axis=1, concat_axis=0, tiled=True)
        solved.append(solved_here)

        def trail_term(offset, amount, source=solved_spread, weights=panel_block):
            return contract(source, weights, 1, 1)

        update = lax.psum_scatter(
            trail_term(jnp.int32(0), lax.axis_size("col") * rhs_here),
            "col",
            scatter_dimension=0,
            tiled=True,
        )
        current = current - update
    return jnp.where(row_place == 0, solved[0], jnp.where(row_place == 1, solved[1], current))


def solution(mesh):
    in_specs = (P("col", "row"), P("row", None, "col"))
    out_specs = P("col", "row")
    return jax.shard_map(local, mesh=mesh, in_specs=in_specs, out_specs=out_specs, check_vma=False)
```

profile of v0, /device:TPU:24, one launch (start us, length us, event | category | flops | bytes accessed | tf_op | source)
XLA Modules:
  0.0 576.8 jit_solution(350811541220198381)
XLA Ops:
  6.5 1.8 copy_bitcast_fusion.3
  8.3 8.6 %all-to-all-start = ((f32[48,16,128]{2,0,1:T(8,128)}), f32[48,16,128]{2,0,1:T(8,128)S(1)}, u32[]{:S(2)}, u32[]{:S(2)}) async-start(f32[48,16,128]{2,0,1:T(8,128)} %copy_bitcast_fusion.3), calls=%async_computation | async-start | bytes 786432 | tf_op jit(solution)/shard_map/all_to_all | solution.py:29
  16.9 0.0 reduce-scatter.5.cloned.1.call-start
  16.9 4.1 fusion
  21.0 9.5 %all-to-all-done = f32[48,16,128]{2,0,1:T(8,128)S(1)} async-done(((f32[48,16,128]{2,0,1:T(8,128)}), f32[48,16,128]{2,0,1:T(8,128)S(1)}, u32[]{:S(2)}, u32[]{:S(2)}) %all-to-all-start) | async-done | bytes 393248 | tf_op jit(solution)/shard_map/all_to_all | solution.py:29
  30.6 7.0 %fusion.1 = f32[768,2048]{1,0:T(8,128)} fusion(f32[768,128]{1,0:T(8,128)S(1)} %bitcast.46, f32[2048,128]{1,0:T(8,128)S(1)} %bitcast.44), kind=kOutput, calls=%fused_computation.8 | convolution fusion | flops 2415919104 | bytes 7733248 | tf_op jit(solution)/shard_map/dot_general | solution.py:13
  37.6 0.0 reduce-scatter.5.cloned.1.call-update
  37.6 0.0 all-reduce.3.cloned.1.call-start
  37.7 64.5 %reduce-scatter.5.cloned.1.call-done = f32[48,2048]{1,0:T(8,128)} async-done(((f32[768,2048]{1,0:T(8,128)}), f32[48,2048]{1,0:T(8,128)}) %reduce-scatter.5.cloned.1.call-update) | async-done | bytes 393232 | tf_op jit(solution)/shard_map/reduce_scatter | solution.py:34
  102.1 0.8 broadcast_select_fusion.1
  102.9 0.0 all-reduce.3.cloned.1.call-update
  102.9 0.0 reduce-scatter.7.cloned.1.call-start
  103.0 95.2 %all-reduce.3.cloned.1.call-done = f32[48,2048]{1,0:T(8,128)} async-done(((f32[48,2048]{1,0:T(8,128)}), f32[48,2048]{1,0:T(8,128)}) %all-reduce.3.cloned.1.call-update) | async-done | bytes 393232 | tf_op jit(solution)/shard_map/psum | solution.py:9
  198.1 1.0 copy_bitcast_fusion.2
  199.1 20.6 %all_to_all.76 = f32[48,16,128]{2,0,1:T(8,128)S(1)} all-to-all(f32[48,16,128]{2,0,1:T(8,128)S(1)} %copy_bitcast_fusion.2), channel_id=1, replica_groups=mesh['row'=16,'col'=16] {'col'}, dimensions={1} | all-to-all | bytes 786432 | tf_op jit(solution)/shard_map/all_to_all | solution.py:41
  219.7 7.0 %fusion.2 = f32[768,2048]{1,0:T(8,128)} fusion(f32[768,128]{1,0:T(8,128)S(1)} %bitcast.47, f32[2048,128]{1,0:T(8,128)S(1)} %bitcast.45), kind=kOutput, calls=%fused_computation.9 | convolution fusion | flops 2415919104 | bytes 7733248 | tf_op jit(solution)/shard_map/dot_general | solution.py:13
  226.7 0.0 reduce-scatter.7.cloned.1.call-update
  226.8 0.0 reduce-scatter.9.cloned.1.call-start
  226.8 63.3 %reduce-scatter.7.cloned.1.call-done = f32[48,2048]{1,0:T(8,128)} async-done(((f32[768,2048]{1,0:T(8,128)}), f32[48,2048]{1,0:T(8,128)}) %reduce-scatter.7.cloned.1.call-update) | async-done | bytes 393232 | tf_op jit(solution)/shard_map/reduce_scatter | solution.py:47
  290.1 1.0 sub.6
  291.1 17.9 %all_to_all.77 = f32[48,16,128]{2,0,1:T(8,128)S(1)} all-to-all(f32[48,16,128]{2,0,1:T(8,128)S(1)} %copy_bitcast_fusion.1), channel_id=1, replica_groups=mesh['row'=16,'col'=16] {'col'}, dimensions={1} | all-to-all | bytes 786432 | tf_op jit(solution)/shard_map/all_to_all | solution.py:29
  309.0 7.0 %fusion.3 = f32[768,2048]{1,0:T(8,128)} fusion(f32[768,128]{1,0:T(8,128)S(1)} %bitcast.48, f32[2048,128]{1,0:T(8,128)S(1)} %bitcast.42), kind=kOutput, calls=%fused_computation.10 | convolution fusion | flops 2415919104 | bytes 7733248 | tf_op jit(solution)/shard_map/dot_general | solution.py:13
  316.0 0.0 all-reduce.5.cloned.1.call-start
  316.1 64.5 %reduce-scatter.9.cloned.1.call-done = f32[48,2048]{1,0:T(8,128)} async-done(((f32[768,2048]{1,0:T(8,128)}), f32[48,2048]{1,0:T(8,128)}) %reduce-scatter.9.cloned.1.call-update) | async-done | bytes 393232 | tf_op jit(solution)/shard_map/reduce_scatter | solution.py:34
  380.6 0.8 broadcast_select_fusion
  381.4 0.0 reduce-scatter.11.cloned.1.call-start
  381.4 94.9 %all-reduce.5.cloned.1.call-done = f32[48,2048]{1,0:T(8,128)} async-done(((f32[48,2048]{1,0:T(8,128)}), f32[48,2048]{1,0:T(8,128)}) %all-reduce.5.cloned.1.call-update) | async-done | bytes 393232 | tf_op jit(solution)/shard_map/psum | solution.py:9
  476.4 1.0 copy_bitcast_fusion
  477.4 20.6 %all_to_all.78 = f32[48,16,128]{2,0,1:T(8,128)S(1)} all-to-all(f32[48,16,128]{2,0,1:T(8,128)S(1)} %copy_bitcast_fusion), channel_id=1, replica_groups=mesh['row'=16,'col'=16] {'col'}, dimensions={1} | all-to-all | bytes 786432 | tf_op jit(solution)/shard_map/all_to_all | solution.py:41
  498.0 7.0 %fusion.4 = f32[768,2048]{1,0:T(8,128)} fusion(f32[768,128]{1,0:T(8,128)S(1)} %bitcast.49, f32[2048,128]{1,0:T(8,128)S(1)} %bitcast.43), kind=kOutput, calls=%fused_computation.11 | convolution fusion | flops 2415919104 | bytes 7733248 | tf_op jit(solution)/shard_map/dot_general | solution.py:13
  505.0 63.2 %reduce-scatter.11.cloned.1.call-done = f32[48,2048]{1,0:T(8,128)} async-done(((f32[768,2048]{1,0:T(8,128)}), f32[48,2048]{1,0:T(8,128)}) %reduce-scatter.11.cloned.1.call-update) | async-done | bytes 393232 | tf_op jit(solution)/shard_map/reduce_scatter | solution.py:47
  568.2 1.8 select_select_fusion
  (10 shorter events, 0.1 us)
Async XLA Ops:
  8.3 22.3 %all-to-all-start = ((f32[48,16,128]{2,0,1:T(8,128)}), f32[48,16,128]{2,0,1:T(8,128)S(1)}, u32[]{:S(2)}, u32[]{:S(2)}) async-start(f32[48,16,128]{2,0,1:T(8,128)} %copy_bitcast_fusion.3), calls=%async_computation | async-start | bytes 786432 | tf_op jit(solution)/shard_map/all_to_all | solution.py:29
  16.9 85.2 %reduce-scatter.5.cloned.1.call-start = ((), (), s32[]{:S(2)}) async-start(), calls=%async_computation.8 | async-start | bytes 6684672 | tf_op jit(solution)/shard_map/reduce_scatter | solution.py:34
  37.6 160.5 %all-reduce.3.cloned.1.call-start = ((), (), s32[]{:S(2)}) async-start(), calls=%async_computation.9 | async-start | bytes 786432 | tf_op jit(solution)/shard_map/psum | solution.py:9
  102.9 187.2 %reduce-scatter.7.cloned.1.call-start = ((), (), s32[]{:S(2)}) async-start(), calls=%async_computation.10 | async-start | bytes 6684672 | tf_op jit(solution)/shard_map/reduce_scatter | solution.py:47
  219.7 70.3 %copy-start.2 = (f32[48,2048]{1,0:T(8,128)S(1)}, f32[48,2048]{1,0:T(8,128)}, u32[]{:S(2)}) copy-start(f32[48,2048]{1,0:T(8,128)} %param.2) | copy-start | bytes 1179652
  226.8 153.8 %reduce-scatter.9.cloned.1.call-start = ((), (), s32[]{:S(2)}) async-start(), calls=%async_computation.11 | async-start | bytes 6684672 | tf_op jit(solution)/shard_map/reduce_scatter | solution.py:34
  316.0 160.4 %all-reduce.5.cloned.1.call-start = ((), (), s32[]{:S(2)}) async-start(), calls=%async_computation.12 | async-start | bytes 786432 | tf_op jit(solution)/shard_map/psum | solution.py:9
  381.4 186.8 %reduce-scatter.11.cloned.1.call-start = ((), (), s32[]{:S(2)}) async-start(), calls=%async_computation.13 | async-start | bytes 6684672 | tf_op jit(solution)/shard_map/reduce_scatter | solution.py:47
  498.0 70.2 %copy-start = (f32[48,2048]{1,0:T(8,128)S(1)}, f32[48,2048]{1,0:T(8,128)}, u32[]{:S(2)}) copy-start(f32[48,2048]{1,0:T(8,128)} %all-reduce.3.cloned.1.call-done) | copy-start | bytes 1179652
  498.0 70.2 %copy-start.1 = (f32[48,2048]{1,0:T(8,128)S(1)}, f32[48,2048]{1,0:T(8,128)}, u32[]{:S(2)}) copy-start(f32[48,2048]{1,0:T(8,128)} %all-reduce.5.cloned.1.call-done) | copy-start | bytes 1179652
Sparse Core Ops, SparseCore 0:
  37.7 64.3 reduce-scatter.4
  105.3 92.7 all-reduce.2
  226.9 63.1 reduce-scatter.6
  316.1 64.4 reduce-scatter.8
  383.7 92.6 all-reduce.4
  505.1 62.9 reduce-scatter.10
where the time goes:
time: 578 us; the launch traced here: 577 us
  waiting for transfers between devices  455 us (79%)
  blocking collectives  59.1 us (10%)
  matrix products  28 us (5%)
  between operations  13.5 us (2%)
  starting transfers between devices  8.82 us (2%)
  local copies, waits for them, and re-layouts  7.94 us (1%)
    psum x2, waiting for transfers between devices, broadcast(): return lax.psum(kept, axis)  190 us
    reduce_scatter x2, waiting for transfers between devices, local(): lax.psum_scatter(solve_term(jnp.int32(0), lax.axis_size('col') * rhs_here...  129 us
    reduce_scatter x2, waiting for transfers between devices, local(): lax.psum_scatter(trail_term(jnp.int32(0), lax.axis_size('col') * rhs_here...  126 us
    all_to_all x2, blocking collectives, local(): lax.all_to_all(solved_here, 'col', split_axis=1, concat_axis=0, tiled=True)  41.2 us
    dot_general x4, matrix products, contract(): lax.dot_general(left, right, (((left_dim,), (right_dim,)), ((), ())), pre...  28 us
    all_to_all x1, blocking collectives, local(): lax.all_to_all(current, 'col', split_axis=1, concat_axis=0, tiled=True)  17.9 us
  transfers between devices with their start and end apart: 7, of which 7 were waited for; matrix products, arithmetic and copies ran while one was open for 1% of the time, Pallas kernels for 0%

commit v1 on v0

v1 whole, which is shorter than its diff:
```python
import jax
import jax.numpy as jnp
from jax import lax
from jax.experimental import pallas as pl
from jax.experimental.pallas import tpu as pltpu
from jax.sharding import PartitionSpec as P

MESH = pl.DeviceIdType.MESH
F32, BF16 = jnp.float32, jnp.bfloat16
NR = 16
NZ = 8
NB = 2048
MB = 48
KB = 128
SUB = 2
HALF = NB // 2
PIECE = HALF // SUB


def split(x):
    hi = x.astype(BF16)
    return hi, (x - hi.astype(F32)).astype(BF16)


def dot_nt(a, b):
    return lax.dot_general(a, b, (((1,), (1,)), ((), ())), preferred_element_type=F32)


def remote(src, dst, ssem, rsem, dev):
    return pltpu.make_async_remote_copy(
        src_ref=src, dst_ref=dst, send_sem=ssem, recv_sem=rsem, device_id=dev, device_id_type=MESH
    )


def loop(lo, hi, body):
    def step(i, carry):
        body(i)
        return carry

    lax.fori_loop(lo, hi, step, 0)


def kernel(
    rhs_hbm, fac_hbm, out_ref,
    fac, rhs, own, other, lhi, llo, w, wb, xs, r1, xb, t, tb, acc, slots,
    loc_sem, s_sc, r_sc, s_z, r_z, s_cx, r_cx, s_ag, r_ag, s_a, r_a, s_l, r_l, s_rs, r_rs,
):
    r = lax.axis_index("row")
    c = lax.axis_index("col")
    z = c // 2
    core = c % 2
    mate = (r, c + 1 - 2 * core)

    def rowpeer(d):
        return (r + d) % NR

    def zpeer(d):
        return (z + d) % NZ

    fac_in = pltpu.make_async_copy(fac_hbm, fac, loc_sem.at[0])
    rhs_in = pltpu.make_async_copy(rhs_hbm, rhs, loc_sem.at[1])
    fac_in.start()
    rhs_in.start()

    barrier = pltpu.get_barrier_semaphore()

    def greet_row(d):
        pl.semaphore_signal(barrier, inc=1, device_id=(rowpeer(d), c), device_id_type=MESH)

    def greet_z(d):
        pl.semaphore_signal(barrier, inc=1, device_id=(r, 2 * zpeer(d) + core), device_id_type=MESH)

    loop(1, NR, greet_row)
    loop(1, NZ, greet_z)
    pl.semaphore_signal(barrier, inc=1, device_id=mate, device_id_type=MESH)

    rhs_in.wait()
    fac_in.wait()

    def compact(i):
        for q in range(2):
            own[q, pl.ds(pl.multiple_of(i * 256, 256), 256), :] = fac[pl.ds(i * 512 + q, 256, stride=2), :]

    loop(0, NB // 256, compact)
    pl.semaphore_wait(barrier, NR - 1 + NZ - 1 + 1)

    def cols(p):
        return pl.ds(pl.multiple_of(p * KB, KB), KB)

    def sc_rhs(panel, p):
        dst = xs.at[0, p] if panel == 0 else r1
        return remote(rhs.at[:, cols(p)], dst, s_sc.at[0, p], r_sc.at[0 if panel == 0 else 1], (p, c))

    def sc_fac(which, p):
        return remote(own.at[which // 2, cols(p)], w.at[which, c], s_sc.at[1 + which // 2, p], r_sc.at[2 + which], (p, c))

    @pl.when(r == 0)
    def _():
        loop(1, NR, lambda d: sc_rhs(0, rowpeer(d)).start())
        loop(1, NR, lambda d: sc_fac(0, rowpeer(d)).start())
        xs[0, 0] = rhs[:, 0:KB]
        w[0, c] = own[0, 0:KB, :]

    @pl.when(r == 1)
    def _():
        loop(1, NR, lambda d: sc_fac(1, rowpeer(d)).start())
        loop(1, NR, lambda d: sc_rhs(1, rowpeer(d)).start())
        loop(1, NR, lambda d: sc_fac(2, rowpeer(d)).start())
        r1[...] = rhs[:, KB : 2 * KB]
        w[1, c] = own[0, KB : 2 * KB, :]
        w[2, c] = own[1, KB : 2 * KB, :]

    def swap(q):
        return remote(own.at[q], other.at[q], s_l.at[q], r_l.at[q], mate)

    for q in range(2):
        swap(q).start()

    def convert(src, lane):
        def step(i):
            at = pl.ds(pl.multiple_of(i * 256, 256), 256)
            for q in range(2):
                hi, lo = split(src[q, at, :])
                lhi[q, at, pl.ds(pl.multiple_of(lane * KB, KB), KB)] = hi
                llo[q, at, pl.ds(pl.multiple_of(lane * KB, KB), KB)] = lo

        loop(0, NB // 256, step)

    convert(own, core)

    def ag(b, d):
        return remote(xs.at[b, r], xs.at[b, r], s_ag.at[b, d], r_ag.at[b, r], (rowpeer(d), c))

    def ag_in(b, d):
        p = rowpeer(d)
        return remote(xs.at[b, p], xs.at[b, p], s_ag.at[b, d], r_ag.at[b, p], (p, c))

    def ag_start(b):
        loop(1, NR, lambda d: ag(b, d).start())

    def ag_wait(b):
        loop(1, NR, lambda d: ag_in(b, d).wait_recv())

    def zsend(q, d):
        return remote(w.at[q, c], w.at[q, c], s_z.at[q, d], r_z.at[q, z], (r, 2 * zpeer(d) + core))

    def zrecv(q, d):
        k = 2 * zpeer(d) + core
        return remote(w.at[q, k], w.at[q, k], s_z.at[q, d], r_z.at[q, zpeer(d)], (r, k))

    def xsend(q, d):
        k = 2 * zpeer(d) + core
        return remote(w.at[q, k], w.at[q, k], s_cx.at[q, d], r_cx.at[q, zpeer(d)], mate)

    def xrecv(q, d):
        k = 2 * zpeer(d) + 1 - core
        return remote(w.at[q, k], w.at[q, k], s_cx.at[q, d], r_cx.at[q, zpeer(d)], mate)

    def ready(q, k):
        hi, lo = split(w[q, k])
        at = cols(k)
        wb[q, 0:KB, at] = hi
        wb[q, KB : 2 * KB, at] = lo

    def fetch(q):
        @pl.when(r != q - q // 2)
        def _():
            remote(w.at[q, c], w.at[q, c], s_sc.at[1, 0], r_sc.at[2 + q], (rowpeer(1), c)).wait_recv()

        loop(1, NZ, lambda d: zsend(q, d).start())
        xsend(q, 0).start()
        ready(q, c)

    def forward(q, lo, hi):
        def step(i):
            h = (i + 2) // 2
            d = h + i % 2 * (NZ - 2 * h)
            zrecv(q, d).wait_recv()
            xsend(q, d).start()
            ready(q, 2 * zpeer(d) + core)

        loop(lo, hi, step)

    def collect(q):
        def step(d):
            xrecv(q, d).wait_recv()
            ready(q, 2 * zpeer(d) + 1 - core)

        loop(0, NZ, step)

    def load_x(b):
        def step(k):
            hi, lo = split(xs[b, k])
            xb[0:MB, cols(k)] = hi
            xb[MB : 2 * MB, cols(k)] = lo

        loop(0, NR, step)

    def product(q):
        o = dot_nt(xb[...], wb[q])
        return o[0:MB, 0:KB] + o[MB : 2 * MB, 0:KB] + o[0:MB, KB : 2 * KB]

    @pl.when(r != 0)
    def _():
        remote(xs.at[0, r], xs.at[0, r], s_sc.at[0, 0], r_sc.at[0], (rowpeer(1), c)).wait_recv()

    ag_start(0)
    fetch(0)
    for q in range(2):
        swap(q).wait_recv()
    convert(other, 1 - core)
    ag_wait(0)
    load_x(0)
    forward(0, 0, 5)
    fetch(1)
    forward(0, 5, 7)
    collect(0)
    xs[1, r] = product(0)
    ag_start(1)
    forward(1, 0, 5)
    fetch(2)
    forward(1, 5, 7)
    collect(1)
    ag_wait(1)
    load_x(1)

    @pl.when(r != 1)
    def _():
        remote(r1, r1, s_sc.at[0, 0], r_sc.at[1], (rowpeer(1), c)).wait_recv()

    xs[2, r] = r1[...] - product(1)
    ag_start(2)

    def a2a(q, d):
        p = zpeer(d)
        return remote(xs.at[1 + 2 * q, pl.ds(2 * p, 2)], t.at[q, z], s_a.at[q, d], r_a.at[q, z], (r, 2 * p + core))

    def a2a_in(q, d):
        p = zpeer(d)
        return remote(t.at[q, p], t.at[q, p], s_a.at[q, d], r_a.at[q, p], (r, 2 * p + core))

    def regroup_start(q):
        loop(1, NZ, lambda d: a2a(q, d).start())
        t[q, z] = xs[1 + 2 * q, pl.ds(2 * z, 2)]

    def regroup_wait(q):
        loop(1, NZ, lambda d: a2a_in(q, d).wait_recv())

    def load_t(q):
        def step(d):
            for k in range(2):
                hi, lo = split(t[q, d, k])
                tb[0, pl.ds(pl.multiple_of(d * MB, MB), MB), k * KB : (k + 1) * KB] = hi
                tb[1, pl.ds(pl.multiple_of(d * MB, MB), MB), k * KB : (k + 1) * KB] = lo

        loop(0, NZ, step)

    regroup_start(0)
    forward(2, 0, 7)
    collect(2)
    ag_wait(2)
    load_x(2)
    xs[3, r] = product(2)
    ag_start(3)
    regroup_wait(0)
    load_t(0)

    def first_part(i):
        at = pl.ds(pl.multiple_of(i * 256, 256), 256)
        hi, lo = tb[0], tb[1]
        o = dot_nt(hi, lhi[0, at, :]) + dot_nt(lo, lhi[0, at, :]) + dot_nt(hi, llo[0, at, :])
        acc[:, :, at] = o.reshape(NZ, MB, 256)

    loop(0, NB // 256, first_part)
    ag_wait(3)
    regroup_start(1)
    regroup_wait(1)
    load_t(1)

    def dest(way, s):
        return (z + NZ - 1 - s) % NZ if way == 0 else (z + 1 + s) % NZ

    def second_part(s):
        for way in range(2):
            d = dest(way, s)
            rows = pl.ds(pl.multiple_of(d * MB, MB), MB)
            hi, lo = tb[0, rows, :], tb[1, rows, :]
            both = jnp.concatenate([hi, lo], axis=0)
            for j in range(HALF // 512):
                at = slice(way * HALF + j * 512, way * HALF + (j + 1) * 512)
                o = dot_nt(both, lhi[1, at, :])
                acc[d, :, at] += o[0:MB] + o[MB : 2 * MB] + dot_nt(hi, llo[1, at, :])

    def hop(way, s, j):
        lanes = pl.ds(way * HALF + j * PIECE, PIECE)
        to = (z + 1) % NZ if way == 0 else (z + NZ - 1) % NZ
        return remote(
            acc.at[dest(way, s), :, lanes], slots.at[way, s, j], s_rs.at[way, s, j], r_rs.at[way, s, j],
            (r, 2 * to + core),
        )

    def take(s):
        for j in range(SUB):
            for way in range(2):
                lanes = slice(way * HALF + j * PIECE, way * HALF + (j + 1) * PIECE)
                hop(way, s, j).wait_recv()
                acc[dest(way, s + 1), :, lanes] += slots[way, s, j]
                yield_send(way, s + 1, j)

    def yield_send(way, s, j):
        @pl.when(s < NZ - 1)
        def _():
            hop(way, s, j).start()

    second_part(0)
    for j in range(SUB):
        for way in range(2):
            hop(way, 0, j).start()

    def ring(s):
        second_part(s + 1)
        take(s)

    loop(0, NZ - 1, ring)

    @pl.when(r == 0)
    def _():
        for k in range(NR):
            out_ref[:, k * KB : (k + 1) * KB] = xs[1, k]

    @pl.when(r == 1)
    def _():
        for k in range(NR):
            out_ref[:, k * KB : (k + 1) * KB] = xs[3, k]

    @pl.when(r > 1)
    def _():
        out_ref[...] = rhs[...] - acc[z]

    @pl.when(r == 0)
    def _():
        loop(1, NR, lambda d: sc_rhs(0, rowpeer(d)).wait_send())
        loop(1, NR, lambda d: sc_fac(0, rowpeer(d)).wait_send())

    @pl.when(r == 1)
    def _():
        loop(1, NR, lambda d: sc_fac(1, rowpeer(d)).wait_send())
        loop(1, NR, lambda d: sc_rhs(1, rowpeer(d)).wait_send())
        loop(1, NR, lambda d: sc_fac(2, rowpeer(d)).wait_send())

    for q in range(2):
        swap(q).wait_send()
        loop(1, NZ, lambda d, q=q: a2a(q, d).wait_send())
    for q in range(3):
        loop(1, NZ, lambda d, q=q: zsend(q, d).wait_send())
        loop(0, NZ, lambda d, q=q: xsend(q, d).wait_send())
    for b in range(4):
        loop(1, NR, lambda d, b=b: ag(b, d).wait_send())

    def drain(s):
        for way in range(2):
            for j in range(SUB):
                hop(way, s, j).wait_send()

    loop(0, NZ - 1, drain)


def local(right_side, factor):
    rows = factor.shape[0]
    dma = pltpu.SemaphoreType.DMA
    return pl.pallas_call(
        kernel,
        name="panels",
        out_shape=jax.ShapeDtypeStruct((MB, NB), F32),
        in_specs=[pl.BlockSpec(memory_space=pl.ANY)] * 2,
        out_specs=pl.BlockSpec(memory_space=pltpu.VMEM),
        scratch_shapes=[
            pltpu.VMEM((2 * NB, KB), F32),
            pltpu.VMEM((MB, NB), F32),
            pltpu.VMEM((2, NB, KB), F32),
            pltpu.VMEM((2, NB, KB), F32),
            pltpu.VMEM((2, NB, 2 * KB), BF16),
            pltpu.VMEM((2, NB, 2 * KB), BF16),
            pltpu.VMEM((3, 16, KB, KB), F32),
            pltpu.VMEM((3, 2 * KB, NB), BF16),
            pltpu.VMEM((4, NR, MB, KB), F32),
            pltpu.VMEM((MB, KB), F32),
            pltpu.VMEM((2 * MB, NB), BF16),
            pltpu.VMEM((2, NZ, 2, MB, KB), F32),
            pltpu.VMEM((2, NZ * MB, 2 * KB), BF16),
            pltpu.VMEM((NZ, MB, NB), F32),
            pltpu.VMEM((2, NZ - 1, SUB, MB, PIECE), F32),
            dma((2,)),
            dma((3, NR)),
            dma((5,)),
            dma((3, NZ)),
            dma((3, NZ)),
            dma((3, NZ)),
            dma((3, NZ)),
            dma((4, NR)),
            dma((4, NR)),
            dma((2, NZ)),
            dma((2, NZ)),
            dma((2,)),
            dma((2,)),
            dma((2, NZ - 1, SUB)),
            dma((2, NZ - 1, SUB)),
        ],
        compiler_params=pltpu.CompilerParams(
            collective_id=0, has_side_effects=True, vmem_limit_bytes=50 * 2**20
        ),
    )(right_side, factor.reshape(2 * rows, KB))


def solution(mesh):
    in_specs = (P("col", "row"), P("row", None, "col"))
    out_specs = P("col", "row")
    return jax.shard_map(local, mesh=mesh, in_specs=in_specs, out_specs=out_specs, check_vma=False)
```

time: 578 us -> 135 us (0.23)
  waiting for transfers between devices: 455 us -> 0 us
  Pallas kernels: 0 us -> 130 us
  blocking collectives: 59.1 us -> 0 us
  matrix products: 28 us -> 0 us
  between operations: 13.5 us -> 0.01 us
  starting transfers between devices: 8.82 us -> 0 us
    reduce_scatter x4 -> x0, waiting for transfers between devices: 255 us -> none  [the longest x2 129 us: local(): lax.psum_scatter(solve_term(jnp.int32(0), lax.axis_size('col') * rhs_here...]
    psum x2 -> x0, waiting for transfers between devices: 190 us -> none  [broadcast(): return lax.psum(kept, axis)]
    pallas_call x0 -> x1, Pallas kernels: none -> 130 us  [local(): pl.pallas_call(kernel, name='panels', out_shape=jax.ShapeDtypeStruct((MB,...]
    all_to_all x3 -> x0, blocking collectives: 59.1 us -> none  [the longest x2 41.2 us: local(): lax.all_to_all(solved_here, 'col', split_axis=1, concat_axis=0, tiled=True)]
    dot_general x4 -> x0, matrix products: 28 us -> none  [contract(): lax.dot_general(left, right, (((left_dim,), (right_dim,)), ((), ())), pre...]
    all_to_all x1 -> x0, waiting for transfers between devices: 9.53 us -> none  [local(): lax.all_to_all(current, 'col', split_axis=1, concat_axis=0, tiled=True)]
    all_to_all x1 -> x0, starting transfers between devices: 8.57 us -> none  [local(): lax.all_to_all(current, 'col', split_axis=1, concat_axis=0, tiled=True)]
  transfers between devices with their start and end apart: 7 -> 0, of which waited for: 7 -> 0; matrix products, arithmetic and copies ran while one was open for 1% -> 0% of each run, Pallas kernels for 0% -> 0%
where the time goes in v1:
time: 135 us; the launch traced here: 134 us
  Pallas kernels  130 us (96%)
  local copies, waits for them, and re-layouts  3.33 us (2%)
    pallas_call x1, Pallas kernels, local(): pl.pallas_call(kernel, name='panels', out_shape=jax.ShapeDtypeStruct((MB,...  130 us
    unnamed x5, local copies, waits for them, and re-layouts  3.33 us

profile of v1, /device:TPU:24, one launch (start us, length us, event | category | flops | bytes accessed | tf_op | source)
XLA Modules:
  0.0 133.6 jit_solution(2047334737299330482)
XLA Ops:
  0.0 0.0 copy-start
  0.0 1.6 %copy-done = f32[2048,2,128]{2,1,0:T(2,128)S(1)} copy-done((f32[2048,2,128]{2,1,0:T(2,128)S(1)}, f32[2048,2,128]{2,1,0:T(2,128)}, u32[]{:S(2)}) %copy-start) | copy-done | bytes 2097176
  1.6 0.0 copy-start.1
  1.6 1.0 copy-done.1
  2.6 130.2 %panels.1 = f32[48,2048]{1,0:T(8,128)S(1)} custom-call(f32[48,2048]{1,0:T(8,128)S(1)} %copy-done.1, f32[4096,128]{1,0:T(8,128)S(1)} %bitcast.1), custom_call_target="tpu_custom_call" | custom-call | tf_op jit(solution)/shard_map/panels/pallas_call | solution.py:371
  132.8 0.7 copy.4
Async XLA Ops:
  0.0 1.6 %copy-start = (f32[2048,2,128]{2,1,0:T(2,128)S(1)}, f32[2048,2,128]{2,1,0:T(2,128)}, u32[]{:S(2)}) copy-start(f32[2048,2,128]{2,1,0:T(2,128)} %param.3) | copy-start | bytes 6291460
  1.6 1.0 copy-start.1

commit v2 on v1

v2 whole, which is shorter than its diff:
```python
import jax
import jax.numpy as jnp
from jax import lax
from jax.experimental import pallas as pl
from jax.experimental.pallas import tpu as pltpu
from jax.sharding import PartitionSpec as P

STOP = 99
MESH = pl.DeviceIdType.MESH
F32, BF16 = jnp.float32, jnp.bfloat16
NR = 16
NX = 4
NZ = 8
NB = 2048
MB = 48
KB = 128
MC = NZ * MB
SUB = 2
HALF = NB // 2
PIECE = HALF // SUB


def split(x):
    hi = x.astype(BF16)
    return hi, (x - hi.astype(F32)).astype(BF16)


def dot_nt(a, b):
    return lax.dot_general(a, b, (((1,), (1,)), ((), ())), preferred_element_type=F32)


def remote(src, dst, ssem, rsem, dev):
    return pltpu.make_async_remote_copy(
        src_ref=src, dst_ref=dst, send_sem=ssem, recv_sem=rsem, device_id=dev, device_id_type=MESH
    )


def loop(lo, hi, body):
    def step(i, carry):
        body(i)
        return carry

    lax.fori_loop(lo, hi, step, 0)


def kernel(
    rhs_hbm, fac_hbm, out_ref,
    fac, rhs, own, other, lhi, llo, w, rel, wb, xs, r1, xb, t, py, pz, gx, s1t, tb, acc, slots,
    loc_sem, s_rhs, r_rhs, s_sc, r_sc, s_rel, r_rel, s_z, r_z, s_cx, r_cx, s_ag, r_ag, s_a, r_a, s_g, r_g, s_o, r_o,
    s_l, r_l, s_rs, r_rs,
):
    r = lax.axis_index("row")
    c = lax.axis_index("col")
    z = c // 2
    core = c % 2
    mate = (r, c + 1 - 2 * core)

    def rowpeer(d):
        return (r + d) % NR

    def zpeer(d):
        return (z + d) % NZ

    fac_in = pltpu.make_async_copy(fac_hbm, fac, loc_sem.at[0])
    rhs_in = pltpu.make_async_copy(rhs_hbm, rhs, loc_sem.at[1])
    fac_in.start()
    rhs_in.start()

    barrier = pltpu.get_barrier_semaphore()

    def greet_row(d):
        pl.semaphore_signal(barrier, inc=1, device_id=(rowpeer(d), c), device_id_type=MESH)

    def greet_z(d):
        pl.semaphore_signal(barrier, inc=1, device_id=(r, 2 * zpeer(d) + core), device_id_type=MESH)

    loop(1, NR, greet_row)
    loop(1, NZ, greet_z)
    pl.semaphore_signal(barrier, inc=1, device_id=mate, device_id_type=MESH)

    rhs_in.wait()
    fac_in.wait()

    def compact(i):
        for q in range(2):
            own[q, i] = fac[pl.ds(i * 512 + q, 256, stride=2), :].reshape(16, 16, KB)

    loop(0, NZ, compact)
    py[...] = jnp.zeros_like(py)
    pl.semaphore_wait(barrier, NR - 1 + NZ - 1 + 1)

    def cols(p):
        return pl.ds(pl.multiple_of(p * KB, KB), KB)

    def slice_of(which, p, h):
        if which == 2:
            return own.at[1, pl.ds(4 * h, 4), p]
        return own.at[0, p // 2, pl.ds(p % 2 * 8 + 4 * h, 4)]

    def half(q, k, h):
        return w.at[q, k, pl.ds(4 * h, 4)]

    def sc_rhs(panel, p):
        dst = xs.at[0, p] if panel == 0 else r1
        return remote(rhs.at[:, cols(p)], dst, s_rhs.at[p], r_rhs.at[panel], (p, c))

    def source(which):
        return 0 if which == 0 else 1

    def far(which, p):
        return jnp.logical_and(p // NX == 2, p % NX != source(which))

    def sc_fac(which, p, h):
        return remote(slice_of(which, p, h), half(which, c, h), s_sc.at[which, h, p], r_sc.at[which, h], (p, c))

    def sc_far(which, p, h):
        to = rel.at[which, pl.ds(4 * h, 4)]
        return remote(slice_of(which, p, h), to, s_sc.at[which, h, p], r_rel.at[which, h], (p % NX, c))

    def relay(which, h):
        got = rel.at[which, pl.ds(4 * h, 4)]
        return remote(got, half(which, c, h), s_rel.at[which, h], r_sc.at[which, h], ((r + 2 * NX) % NR, c))

    def sc_fac_go(which, h, act):
        def step(d):
            p = rowpeer(d)
            f = far(which, p)

            @pl.when(f)
            def _():
                act(sc_far(which, p, h))

            @pl.when(jnp.logical_not(f))
            def _():
                act(sc_fac(which, p, h))

        loop(1, NR, step)

    def sc_fac_start(which):
        for h in range(2):
            sc_fac_go(which, h, lambda cp: cp.start())

    def sc_fac_left(which):
        for h in range(2):
            sc_fac_go(which, h, lambda cp: cp.wait_send())

    def is_relay(which):
        return jnp.logical_and(r < NX, r != source(which))

    def relay_go(which, h):
        @pl.when(is_relay(which))
        def _():
            got = rel.at[which, pl.ds(4 * h, 4)]
            remote(got, got, s_rel.at[which, h], r_rel.at[which, h], (rowpeer(1), c)).wait_recv()
            relay(which, h).start()

    def rhs_start(panel):
        @pl.when(r == panel)
        def _():
            loop(1, NR, lambda d: sc_rhs(panel, rowpeer(d)).start())

    def last_start():
        @pl.when(r == 1)
        def _():
            sc_fac_start(2)

    @pl.when(r == 0)
    def _():
        sc_fac_start(0)
        xs[0, 0] = rhs[:, 0:KB]
        w[0, c] = own[0, 0, 0:8]

    @pl.when(r == 1)
    def _():
        sc_fac_start(1)
        r1[...] = rhs[:, KB : 2 * KB]
        w[1, c] = own[0, 0, 8:16]
        w[2, c] = own[1, :, 1]

    def swap(q):
        return remote(own.at[q], other.at[q], s_l.at[q], r_l.at[q], mate)

    for q in range(2):
        swap(q).start()

    def convert(src, lane):
        def step(i):
            at = pl.ds(pl.multiple_of(i * 256, 256), 256)
            for q in range(2):
                hi, lo = split(src[q, i].reshape(256, KB))
                lhi[q, at, cols(lane)] = hi
                llo[q, at, cols(lane)] = lo

        loop(0, NZ, step)

    def ag(b, d):
        return remote(xs.at[b, r], xs.at[b, r], s_ag.at[b, d], r_ag.at[b, r], (rowpeer(d), c))

    def ag_in(b, d):
        p = rowpeer(d)
        return remote(xs.at[b, p], xs.at[b, p], s_ag.at[b, d], r_ag.at[b, p], (p, c))

    def ag_start(b):
        loop(1, NR, lambda d: ag(b, d).start())

    def ag_wait(b):
        loop(1, NR, lambda d: ag_in(b, d).wait_recv())

    def zcopy(q, h, i, far_z, d):
        k = 2 * far_z + core
        return remote(half(q, k, h), half(q, k, h), s_z.at[q, h, i], r_z.at[q, h, far_z], (r, 2 * zpeer(d) + core))

    def zfirst(q, h):
        return [zcopy(q, h, i, z, d) for i, d in enumerate((2, NZ - 2, 1, NZ - 1))]

    def zsecond(q, h):
        left, right = zpeer(NZ - 2), zpeer(2)
        last = zcopy(q, h, 6, left, 2) if h == 0 else zcopy(q, h, 6, right, NZ - 2)
        return [last, zcopy(q, h, 4, left, 1), zcopy(q, h, 5, right, NZ - 1)]

    def zin(q, h, d):
        zcopy(q, h, 0, zpeer(d), 1).wait_recv()

    def xsend(q, d):
        k = 2 * zpeer(d) + core
        return remote(w.at[q, k], w.at[q, k], s_cx.at[q, d], r_cx.at[q, zpeer(d)], mate)

    def xrecv(q, d):
        k = 2 * zpeer(d) + 1 - core
        return remote(w.at[q, k], w.at[q, k], s_cx.at[q, d], r_cx.at[q, zpeer(d)], mate)

    def ready(q, k):
        hi, lo = split(w[q, k].reshape(KB, KB))
        at = cols(k)
        wb[q, 0:KB, at] = hi
        wb[q, KB : 2 * KB, at] = lo

    def slice_in(q, h):
        @pl.when(r != source(q))
        def _():
            remote(half(q, c, h), half(q, c, h), s_rhs.at[0], r_sc.at[q, h], (rowpeer(1), c)).wait_recv()

    def fetch(q):
        for h in range(2):
            relay_go(q, h)
            slice_in(q, h)
            for cp in zfirst(q, h):
                cp.start()
        xsend(q, 0).start()
        ready(q, c)

    def hand_on(q, h):
        zin(q, h, 2)
        zin(q, h, NZ - 2)
        for cp in zsecond(q, h):
            cp.start()

    def near(q):
        for d in (2, NZ - 2):
            xsend(q, d).start()
            ready(q, 2 * zpeer(d) + core)
        arrive(q, (1, NZ - 1))

    def arrive(q, which):
        for d in which:
            for h in range(2):
                zin(q, h, d)
            xsend(q, d).start()
            ready(q, 2 * zpeer(d) + core)

    def collect(q):
        def step(d):
            xrecv(q, d).wait_recv()
            ready(q, 2 * zpeer(d) + 1 - core)

        loop(0, NZ, step)

    def load_x(b):
        def step(k):
            hi, lo = split(xs[b, k])
            xb[0:MB, cols(k)] = hi
            xb[MB : 2 * MB, cols(k)] = lo

        loop(0, NR, step)

    def product(q):
        o = dot_nt(xb[...], wb[q])
        return o[0:MB, 0:KB] + o[MB : 2 * MB, 0:KB] + o[0:MB, KB : 2 * KB]

    def rhs0_in():
        @pl.when(r != 0)
        def _():
            remote(xs.at[0, r], xs.at[0, r], s_rhs.at[0], r_rhs.at[0], (rowpeer(1), c)).wait_recv()

    def rhs1_in():
        @pl.when(r != 1)
        def _():
            remote(r1, r1, s_rhs.at[0], r_rhs.at[1], (rowpeer(1), c)).wait_recv()

    def swap_in():
        for q in range(2):
            swap(q).wait_recv()

    def a2a(d):
        p = zpeer(d)
        return remote(xs.at[1, pl.ds(2 * p, 2)], t.at[z], s_a.at[0, d], r_a.at[0, z], (r, 2 * p + core))

    def a2a_in(d):
        p = zpeer(d)
        return remote(t.at[p], t.at[p], s_a.at[0, d], r_a.at[0, p], (r, 2 * p + core))

    def regroup(d):
        p = zpeer(d)
        return remote(py.at[p], pz.at[z], s_a.at[1, d], r_a.at[1, z], (r, 2 * p + core))

    def regroup_in(d):
        p = zpeer(d)
        return remote(pz.at[p], pz.at[p], s_a.at[1, d], r_a.at[1, p], (r, 2 * p + core))

    def spread(g, d):
        return remote(gx.at[g, r], gx.at[g, r], s_g.at[g, d], r_g.at[g, r], (rowpeer(d), c))

    def spread_in(g, d):
        p = rowpeer(d)
        return remote(gx.at[g, p], gx.at[g, p], s_g.at[g, d], r_g.at[g, p], (p, c))

    def to_owner():
        return remote(py, s1t.at[:, r], s_o, r_o.at[r], (1, c))

    def from_peer(d):
        p = rowpeer(d)
        return remote(py, s1t.at[:, p], s_o, r_o.at[p], (p, c))

    def dest(way, s):
        return (z + NZ - 1 - s) % NZ if way == 0 else (z + 1 + s) % NZ

    def hop(way, s, j):
        lanes = pl.ds(way * HALF + j * PIECE, PIECE)
        to = (z + 1) % NZ if way == 0 else (z + NZ - 1) % NZ
        return remote(
            acc.at[dest(way, s), :, lanes], slots.at[way, s, j], s_rs.at[way, s, j], r_rs.at[way, s, j],
            (r, 2 * to + core),
        )

    def left_scatter():
        @pl.when(r == 0)
        def _():
            loop(1, NR, lambda d: sc_rhs(0, rowpeer(d)).wait_send())
            sc_fac_left(0)

        @pl.when(r == 1)
        def _():
            loop(1, NR, lambda d: sc_rhs(1, rowpeer(d)).wait_send())
            sc_fac_left(1)
            sc_fac_left(2)

        for which in range(3):

            @pl.when(is_relay(which))
            def _(which=which):
                for h in range(2):
                    relay(which, h).wait_send()

    def left_swap():
        for q in range(2):
            swap(q).wait_send()

    def left_f(q):
        for h in range(2):
            for cp in zfirst(q, h) + zsecond(q, h):
                cp.wait_send()
        loop(0, NZ, lambda d: xsend(q, d).wait_send())

    def left_ag(b):
        loop(1, NR, lambda d: ag(b, d).wait_send())

    def left_a2a():
        loop(1, NZ, lambda d: a2a(d).wait_send())

    def left_regroup():
        loop(1, NZ, lambda d: regroup(d).wait_send())

    def left_spread():
        for g in range(4):
            loop(1, NR, lambda d, g=g: spread(g, d).wait_send())

    def left_ring():
        def drain(s):
            for way in range(2):
                for j in range(SUB):
                    hop(way, s, j).wait_send()

        loop(0, NZ - 1, drain)

    convert(own, core)
    fetch(0)
    rhs_start(0)
    fetch(1)
    rhs0_in()
    ag_start(0)
    hand_on(0, 0)
    hand_on(0, 1)
    last_start()
    near(0)
    hand_on(1, 0)
    hand_on(1, 1)
    arrive(0, (3, NZ - 3, 4))
    rhs_start(1)
    near(1)
    fetch(2)
    ag_wait(0)
    load_x(0)
    collect(0)
    xs[1, r] = product(0)
    ag_start(1)
    hand_on(2, 0)
    hand_on(2, 1)
    arrive(1, (3, NZ - 3, 4))
    swap_in()
    convert(other, 1 - core)
    near(2)
    arrive(2, (3, NZ - 3, 4))
    ag_wait(1)
    load_x(1)
    loop(1, NZ, lambda d: a2a(d).start())
    t[z] = xs[1, pl.ds(2 * z, 2)]
    collect(1)
    rhs1_in()
    xs[2, r] = r1[...] - product(1)
    ag_start(2)
    ag_wait(2)
    collect(2)
    load_x(2)
    turned = dot_nt(wb[2], xb[0:MB, :])
    turned = turned[0:KB] + turned[KB : 2 * KB] + dot_nt(wb[2, 0:KB, :], xb[MB : 2 * MB, :])
    py[:, :, 0:MB] = turned.reshape(NZ, 16, MB)
    loop(1, NZ, lambda d: regroup(d).start())
    pz[z] = py[z]

    @pl.when(r != 1)
    def _():
        to_owner().start()

    @pl.when(r == 1)
    def _():
        s1t[:, 1] = py[...]

    loop(1, NZ, lambda d: a2a_in(d).wait_recv())

    def load_t(d):
        for k in range(2):
            hi, lo = split(t[d, k])
            tb[0, pl.ds(pl.multiple_of(d * MB, MB), MB), k * KB : (k + 1) * KB] = hi
            tb[1, pl.ds(pl.multiple_of(d * MB, MB), MB), k * KB : (k + 1) * KB] = lo

    loop(0, NZ, load_t)

    def first_part(i):
        at = pl.ds(pl.multiple_of(i * 256, 256), 256)
        hi, lo = tb[0], tb[1]
        o = dot_nt(hi, lhi[0, at, :]) + dot_nt(lo, lhi[0, at, :]) + dot_nt(hi, llo[0, at, :])
        acc[:, :, at] = o.reshape(NZ, MB, 256)

    loop(1, NZ, lambda d: regroup_in(d).wait_recv())

    def pair(g):
        return (z + NZ - 1 - g) % NZ, z if g == 3 else (z + 1 + g) % NZ

    def spread_start(g):
        one, two = pair(g)
        gx[g, r] = pz[one] + pltpu.roll(pz[two], MB, 1)
        loop(1, NR, lambda d: spread(g, d).start())

    def spread_end(g):
        loop(1, NR, lambda d: spread_in(g, d).wait_recv())
        for k in range(2):
            hi, lo = split(gx[g, 8 * k : 8 * k + 8].reshape(KB, KB).T)
            for i, d in enumerate(pair(g)):
                rows = pl.ds(pl.multiple_of(d * MB, MB), MB)
                tb[0, rows, k * KB : (k + 1) * KB] = hi[i * MB : (i + 1) * MB]
                tb[1, rows, k * KB : (k + 1) * KB] = lo[i * MB : (i + 1) * MB]

    spread_start(0)
    loop(0, NB // 256, first_part)
    spread_end(0)

    def second_part(s):
        for way in range(2):
            d = dest(way, s)
            rows = pl.ds(pl.multiple_of(d * MB, MB), MB)
            hi, lo = tb[0, rows, :], tb[1, rows, :]
            both = jnp.concatenate([hi, lo], axis=0)
            for j in range(HALF // 512):
                at = slice(way * HALF + j * 512, way * HALF + (j + 1) * 512)
                o = dot_nt(both, lhi[1, at, :])
                acc[d, :, at] += o[0:MB] + o[MB : 2 * MB] + dot_nt(hi, llo[1, at, :])

    def pass_on(way, s, j):
        @pl.when(jnp.int32(s) < NZ - 1)
        def _():
            hop(way, s, j).start()

    def ring(s):
        if isinstance(s, int) and s < 3:
            spread_end(s + 1)
            if s < 2:
                spread_start(s + 2)
        second_part(s + 1)
        for j in range(SUB):
            for way in range(2):
                lanes = slice(way * HALF + j * PIECE, way * HALF + (j + 1) * PIECE)
                hop(way, s, j).wait_recv()
                acc[dest(way, s + 1), :, lanes] += slots[way, s, j]
                pass_on(way, s + 1, j)

    second_part(0)
    for j in range(SUB):
        for way in range(2):
            hop(way, 0, j).start()
    spread_start(1)
    for s in range(3):
        ring(s)
    loop(3, NZ - 1, ring)

    @pl.when(r == 0)
    def _():
        for k in range(NR):
            out_ref[:, k * KB : (k + 1) * KB] = xs[1, k]

    @pl.when(r == 1)
    def _():
        loop(1, NR, lambda d: from_peer(d).wait_recv())
        for k in range(NR):
            block = s1t[k // 2, k % 2 * 8 : k % 2 * 8 + 8].reshape(KB, KB)
            out_ref[:, k * KB : (k + 1) * KB] = block.T[0:MB]

    @pl.when(r > 1)
    def _():
        out_ref[...] = rhs[...] - acc[z]

    @pl.when(r != 1)
    def _():
        to_owner().wait_send()

    left_scatter()
    left_swap()
    for q in range(3):
        left_f(q)
        left_ag(q)
    left_a2a()
    left_regroup()
    left_spread()
    left_ring()


def local(right_side, factor):
    rows = factor.shape[0]
    dma = pltpu.SemaphoreType.DMA
    return pl.pallas_call(
        kernel,
        name="panels",
        out_shape=jax.ShapeDtypeStruct((MB, NB), F32),
        in_specs=[pl.BlockSpec(memory_space=pl.ANY)] * 2,
        out_specs=pl.BlockSpec(memory_space=pltpu.VMEM),
        scratch_shapes=[
            pltpu.VMEM((2 * NB, KB), F32),
            pltpu.VMEM((MB, NB), F32),
            pltpu.VMEM((2, NZ, 16, 16, KB), F32),
            pltpu.VMEM((2, NZ, 16, 16, KB), F32),
            pltpu.VMEM((2, NB, 2 * KB), BF16),
            pltpu.VMEM((2, NB, 2 * KB), BF16),
            pltpu.VMEM((3, 16, 8, 16, KB), F32),
            pltpu.VMEM((3, 8, 16, KB), F32),
            pltpu.VMEM((3, 2 * KB, NB), BF16),
            pltpu.VMEM((3, NR, MB, KB), F32),
            pltpu.VMEM((MB, KB), F32),
            pltpu.VMEM((2 * MB, NB), BF16),
            pltpu.VMEM((NZ, 2, MB, KB), F32),
            pltpu.VMEM((NZ, 16, KB), F32),
            pltpu.VMEM((NZ, 16, KB), F32),
            pltpu.VMEM((4, NR, 16, KB), F32),
            pltpu.VMEM((NZ, NR, 16, KB), F32),
            pltpu.VMEM((2, MC, 2 * KB), BF16),
            pltpu.VMEM((NZ, MB, NB), F32),
            pltpu.VMEM((2, NZ - 1, SUB, MB, PIECE), F32),
            dma((2,)),
            dma((NR,)),
            dma((2,)),
            dma((3, 2, NR)),
            dma((3, 2)),
            dma((3, 2)),
            dma((3, 2)),
            dma((3, 2, 7)),
            dma((3, 2, NZ)),
            dma((3, NZ)),
            dma((3, NZ)),
            dma((3, NR)),
            dma((3, NR)),
            dma((2, NZ)),
            dma((2, NZ)),
            dma((4, NR)),
            dma((4, NR)),
            dma,
            dma((NR,)),
            dma((2,)),
            dma((2,)),
            dma((2, NZ - 1, SUB)),
            dma((2, NZ - 1, SUB)),
        ],
        compiler_params=pltpu.CompilerParams(
            collective_id=0, has_side_effects=True, vmem_limit_bytes=60 * 2**20
        ),
    )(right_side, factor.reshape(2 * rows, KB))


def solution(mesh):
    in_specs = (P("col", "row"), P("row", None, "col"))
    out_specs = P("col", "row")
    return jax.shard_map(local, mesh=mesh, in_specs=in_specs, out_specs=out_specs, check_vma=False)
```

time: 135 us -> 114 us (0.84)
  the two profiles are of different devices: /device:TPU:24 before, /device:TPU:8 now
where the time goes in v2:
time: 114 us
  Pallas kernels  112 us (98%)
  local copies, waits for them, and re-layouts  1.77 us (2%)
    pallas_call x1, Pallas kernels, local(): pl.pallas_call(kernel, name='panels', out_shape=jax.ShapeDtypeStruct((MB,...  112 us

profile of v2, /device:TPU:8, one launch (start us, length us, event | category | flops | bytes accessed | tf_op | source)
XLA Modules:
  0.0 114.3 jit_solution(7187916949888068064)
XLA Ops:
  0.0 112.5 %panels.1 = f32[48,2048]{1,0:T(8,128)} custom-call(f32[48,2048]{1,0:T(8,128)} %rhs_hbm.1, f32[4096,128]{1,0:T(8,128)} %bitcast.1), custom_call_target="tpu_custom_call" | custom-call | tf_op jit(solution)/shard_map/panels/pallas_call | solution.py:559
  112.5 1.8 %copy.4 = f32[48,2048]{1,0:T(8,128)} copy(f32[48,2048]{1,0:T(8,128)} %panels.1) | data formatting | bytes 786432

commit v3 on v2

--- a/solution.py
+++ b/solution.py
@@ -45,7 +45,7 @@
 
 def kernel(
     rhs_hbm, fac_hbm, out_ref,
-    fac, rhs, own, other, lhi, llo, w, rel, wb, xs, r1, xb, t, py, pz, gx, s1t, tb, acc, slots,
+    fac, rhs, own, other, lhi, llo, w, rel, wb, xs, r1, xb, t, py, pz, gx, s1t, ta, tb, acc, slots,
     loc_sem, s_rhs, r_rhs, s_sc, r_sc, s_rel, r_rel, s_z, r_z, s_cx, r_cx, s_ag, r_ag, s_a, r_a, s_g, r_g, s_o, r_o,
     s_l, r_l, s_rs, r_rs,
 ):
@@ -68,13 +68,15 @@
 
     barrier = pltpu.get_barrier_semaphore()
 
-    def greet_row(d):
-        pl.semaphore_signal(barrier, inc=1, device_id=(rowpeer(d), c), device_id_type=MESH)
+    def greet_row(p):
+        @pl.when(p != r)
+        def _():
+            pl.semaphore_signal(barrier, inc=1, device_id=(p, c), device_id_type=MESH)
 
     def greet_z(d):
         pl.semaphore_signal(barrier, inc=1, device_id=(r, 2 * zpeer(d) + core), device_id_type=MESH)
 
-    loop(1, NR, greet_row)
+    loop(0, NR, greet_row)
     loop(1, NZ, greet_z)
     pl.semaphore_signal(barrier, inc=1, device_id=mate, device_id_type=MESH)
 
@@ -301,12 +303,16 @@
         for q in range(2):
             swap(q).wait_recv()
 
+    def zorder(i):
+        h = (i + 1) // 2
+        return h + (i + 1) % 2 * (NZ - 2 * h)
+
     def a2a(d):
         p = zpeer(d)
         return remote(xs.at[1, pl.ds(2 * p, 2)], t.at[z], s_a.at[0, d], r_a.at[0, z], (r, 2 * p + core))
 
-    def a2a_in(d):
-        p = zpeer(d)
+    def a2a_from(p):
+        d = 1
         return remote(t.at[p], t.at[p], s_a.at[0, d], r_a.at[0, p], (r, 2 * p + core))
 
     def regroup(d):
@@ -381,8 +387,7 @@
         loop(1, NZ, lambda d: regroup(d).wait_send())
 
     def left_spread():
-        for g in range(4):
-            loop(1, NR, lambda d, g=g: spread(g, d).wait_send())
+        loop(1, NR, lambda d: spread(1, d).wait_send())
 
     def left_ring():
         def drain(s):
@@ -422,12 +427,12 @@
     arrive(2, (3, NZ - 3, 4))
     ag_wait(1)
     load_x(1)
-    loop(1, NZ, lambda d: a2a(d).start())
-    t[z] = xs[1, pl.ds(2 * z, 2)]
     collect(1)
     rhs1_in()
     xs[2, r] = r1[...] - product(1)
     ag_start(2)
+    loop(1, NZ, lambda d: a2a(d).start())
+    t[z] = xs[1, pl.ds(2 * z, 2)]
     ag_wait(2)
     collect(2)
     load_x(2)
@@ -437,63 +442,59 @@
     loop(1, NZ, lambda d: regroup(d).start())
     pz[z] = py[z]
 
-    @pl.when(r != 1)
-    def _():
-        to_owner().start()
-
-    @pl.when(r == 1)
-    def _():
-        s1t[:, 1] = py[...]
-
-    loop(1, NZ, lambda d: a2a_in(d).wait_recv())
-
-    def load_t(d):
+    loop(1, NZ, lambda d: regroup_in(d).wait_recv())
+
+    def pair(g):
+        return (z + NZ - 1 - g) % NZ, z if g == 3 else (z + 1 + g) % NZ
+
+    def spread_start(g):
+        for i in range(2):
+            one, two = pair(2 * g + i)
+            gx[g, r, i] = pz[one] + pltpu.roll(pz[two], MB, 1)
+        loop(1, NR, lambda d: spread(g, d).start())
+
+    def spread_end(g):
+        loop(1, NR, lambda d: spread_in(g, d).wait_recv())
+        for n in range(2):
+            for k in range(2):
+                hi, lo = split(gx[g, 8 * k : 8 * k + 8, n].reshape(KB, KB).T)
+                for i, d in enumerate(pair(2 * g + n)):
+                    rows = pl.ds(pl.multiple_of(d * MB, MB), MB)
+                    tb[0, rows, k * KB : (k + 1) * KB] = hi[i * MB : (i + 1) * MB]
+                    tb[1, rows, k * KB : (k + 1) * KB] = lo[i * MB : (i + 1) * MB]
+
+    spread_start(0)
+
+    def first_in(d, away):
+        if away:
+            a2a_from(d).wait_recv()
+        rows = pl.ds(pl.multiple_of(d * MB, MB), MB)
         for k in range(2):
             hi, lo = split(t[d, k])
-            tb[0, pl.ds(pl.multiple_of(d * MB, MB), MB), k * KB : (k + 1) * KB] = hi
-            tb[1, pl.ds(pl.multiple_of(d * MB, MB), MB), k * KB : (k + 1) * KB] = lo
-
-    loop(0, NZ, load_t)
-
-    def first_part(i):
-        at = pl.ds(pl.multiple_of(i * 256, 256), 256)
-        hi, lo = tb[0], tb[1]
-        o = dot_nt(hi, lhi[0, at, :]) + dot_nt(lo, lhi[0, at, :]) + dot_nt(hi, llo[0, at, :])
-        acc[:, :, at] = o.reshape(NZ, MB, 256)
-
-    loop(1, NZ, lambda d: regroup_in(d).wait_recv())
-
-    def pair(g):
-        return (z + NZ - 1 - g) % NZ, z if g == 3 else (z + 1 + g) % NZ
-
-    def spread_start(g):
-        one, two = pair(g)
-        gx[g, r] = pz[one] + pltpu.roll(pz[two], MB, 1)
-        loop(1, NR, lambda d: spread(g, d).start())
-
-    def spread_end(g):
-        loop(1, NR, lambda d: spread_in(g, d).wait_recv())
-        for k in range(2):
-            hi, lo = split(gx[g, 8 * k : 8 * k + 8].reshape(KB, KB).T)
-            for i, d in enumerate(pair(g)):
-                rows = pl.ds(pl.multiple_of(d * MB, MB), MB)
-                tb[0, rows, k * KB : (k + 1) * KB] = hi[i * MB : (i + 1) * MB]
-                tb[1, rows, k * KB : (k + 1) * KB] = lo[i * MB : (i + 1) * MB]
-
-    spread_start(0)
-    loop(0, NB // 256, first_part)
-    spread_end(0)
-
-    def second_part(s):
+            ta[0, rows, k * KB : (k + 1) * KB] = hi
+            ta[1, rows, k * KB : (k + 1) * KB] = lo
+
+    def first_in_step(s):
+        first_in(dest(0, s), True)
+        first_in(z if s == 3 else dest(1, s), s != 3)
+
+    def part(q, way, s):
+        d = dest(way, s)
+        rows = pl.ds(pl.multiple_of(d * MB, MB), MB)
+        from_ = ta if q == 0 else tb
+        hi, lo = from_[0, rows, :], from_[1, rows, :]
+        for j in range(HALF // 512):
+            at = slice(way * HALF + j * 512, way * HALF + (j + 1) * 512)
+            o = dot_nt(jnp.concatenate([hi, lo], axis=0), lhi[q, at, :])
+            o = o[0:MB] + o[MB : 2 * MB] + dot_nt(hi, llo[q, at, :])
+            if q == 0:
+                acc[d, :, at] = o
+            else:
+                acc[d, :, at] += o
+
+    def parts(q, s):
         for way in range(2):
-            d = dest(way, s)
-            rows = pl.ds(pl.multiple_of(d * MB, MB), MB)
-            hi, lo = tb[0, rows, :], tb[1, rows, :]
-            both = jnp.concatenate([hi, lo], axis=0)
-            for j in range(HALF // 512):
-                at = slice(way * HALF + j * 512, way * HALF + (j + 1) * 512)
-                o = dot_nt(both, lhi[1, at, :])
-                acc[d, :, at] += o[0:MB] + o[MB : 2 * MB] + dot_nt(hi, llo[1, at, :])
+            part(q, way, s)
 
     def pass_on(way, s, j):
         @pl.when(jnp.int32(s) < NZ - 1)
@@ -501,26 +502,51 @@
             hop(way, s, j).start()
 
     def ring(s):
-        if isinstance(s, int) and s < 3:
-            spread_end(s + 1)
-            if s < 2:
-                spread_start(s + 2)
-        second_part(s + 1)
+        if isinstance(s, int) and s == 1:
+            spread_end(1)
+            parts(1, 2)
         for j in range(SUB):
             for way in range(2):
                 lanes = slice(way * HALF + j * PIECE, way * HALF + (j + 1) * PIECE)
                 hop(way, s, j).wait_recv()
                 acc[dest(way, s + 1), :, lanes] += slots[way, s, j]
                 pass_on(way, s + 1, j)
-
-    second_part(0)
-    for j in range(SUB):
-        for way in range(2):
+            if isinstance(s, int) and s == 6:
+                continue
+            if j == 0:
+                if isinstance(s, int) and s < 2:
+                    first_in_step(s + 2)
+                parts(0, s + 2)
+            if j == SUB - 1:
+                if isinstance(s, int) and s == 0:
+                    continue
+                parts(1, s + 2)
+
+    for s in range(2):
+        first_in_step(s)
+        parts(0, s)
+    loop(1, NR, lambda d: spread(0, d).wait_send())
+    spread_start(1)
+    spread_end(0)
+    for way in range(2):
+        part(1, way, 0)
+        for j in range(SUB):
             hop(way, 0, j).start()
-    spread_start(1)
-    for s in range(3):
+    parts(1, 1)
+
+    @pl.when(r != 1)
+    def _():
+        to_owner().start()
+
+    @pl.when(r == 1)
+    def _():
+        s1t[:, 1] = py[...]
+
+
+    for s in range(2):
         ring(s)
-    loop(3, NZ - 1, ring)
+    loop(2, NZ - 2, ring)
+    ring(NZ - 2)
 
     @pl.when(r == 0)
     def _():
@@ -578,8 +604,9 @@
             pltpu.VMEM((NZ, 2, MB, KB), F32),
             pltpu.VMEM((NZ, 16, KB), F32),
             pltpu.VMEM((NZ, 16, KB), F32),
-            pltpu.VMEM((4, NR, 16, KB), F32),
+            pltpu.VMEM((2, NR, 2, 16, KB), F32),
             pltpu.VMEM((NZ, NR, 16, KB), F32),
+            pltpu.VMEM((2, MC, 2 * KB), BF16),
             pltpu.VMEM((2, MC, 2 * KB), BF16),
             pltpu.VMEM((NZ, MB, NB), F32),
             pltpu.VMEM((2, NZ - 1, SUB, MB, PIECE), F32),
@@ -598,8 +625,8 @@
             dma((3, NR)),
             dma((2, NZ)),
             dma((2, NZ)),
-            dma((4, NR)),
-            dma((4, NR)),
+            dma((2, NR)),
+            dma((2, NR)),
             dma,
             dma((NR,)),
             dma((2,)),

time: 114 us -> 111 us (0.974)
  Pallas kernels: 112 us -> 109 us
    pallas_call x1, Pallas kernels: 112 us -> 109 us  [local(): pl.pallas_call(kernel, name='panels', out_shape=jax.ShapeDtypeStruct((MB,...]
where the time goes in v3:
time: 111 us
  Pallas kernels  109 us (98%)
  local copies, waits for them, and re-layouts  1.77 us (2%)
    pallas_call x1, Pallas kernels, local(): pl.pallas_call(kernel, name='panels', out_shape=jax.ShapeDtypeStruct((MB,...  109 us

profile of v3, /device:TPU:8, one launch (start us, length us, event | category | flops | bytes accessed | tf_op | source)
XLA Modules:
  0.0 110.6 jit_solution(14457563333345300164)
XLA Ops:
  0.0 108.8 %panels.1 = f32[48,2048]{1,0:T(8,128)} custom-call(f32[48,2048]{1,0:T(8,128)} %rhs_hbm.1, f32[4096,128]{1,0:T(8,128)} %bitcast.1), custom_call_target="tpu_custom_call" | custom-call | tf_op jit(solution)/shard_map/panels/pallas_call | solution.py:585
  108.8 1.8 %copy.4 = f32[48,2048]{1,0:T(8,128)} copy(f32[48,2048]{1,0:T(8,128)} %panels.1) | data formatting | bytes 786432

commit v4 on v3

--- a/solution.py
+++ b/solution.py
@@ -15,7 +15,7 @@
 MB = 48
 KB = 128
 MC = NZ * MB
-SUB = 2
+SUB = 4
 HALF = NB // 2
 PIECE = HALF // SUB
 
@@ -389,28 +389,25 @@
     def left_spread():
         loop(1, NR, lambda d: spread(1, d).wait_send())
 
-    def left_ring():
-        def drain(s):
-            for way in range(2):
-                for j in range(SUB):
-                    hop(way, s, j).wait_send()
-
-        loop(0, NZ - 1, drain)
+    def drain(s):
+        for way in range(2):
+            for j in range(SUB):
+                hop(way, s, j).wait_send()
 
     convert(own, core)
     fetch(0)
     rhs_start(0)
     fetch(1)
+    last_start()
+    rhs_start(1)
+    hand_on(0, 0)
+    hand_on(0, 1)
     rhs0_in()
     ag_start(0)
-    hand_on(0, 0)
-    hand_on(0, 1)
-    last_start()
     near(0)
     hand_on(1, 0)
     hand_on(1, 1)
     arrive(0, (3, NZ - 3, 4))
-    rhs_start(1)
     near(1)
     fetch(2)
     ag_wait(0)
@@ -433,6 +430,10 @@
     ag_start(2)
     loop(1, NZ, lambda d: a2a(d).start())
     t[z] = xs[1, pl.ds(2 * z, 2)]
+    left_swap()
+    for q in range(2):
+        left_f(q)
+        left_ag(q)
     ag_wait(2)
     collect(2)
     load_x(2)
@@ -442,6 +443,8 @@
     loop(1, NZ, lambda d: regroup(d).start())
     pz[z] = py[z]
 
+    left_f(2)
+    left_ag(2)
     loop(1, NZ, lambda d: regroup_in(d).wait_recv())
 
     def pair(g):
@@ -511,6 +514,8 @@
                 hop(way, s, j).wait_recv()
                 acc[dest(way, s + 1), :, lanes] += slots[way, s, j]
                 pass_on(way, s + 1, j)
+            if j == 1 and not (isinstance(s, int) and s == 0):
+                drain(s - 1)
             if isinstance(s, int) and s == 6:
                 continue
             if j == 0:
@@ -528,55 +533,53 @@
     loop(1, NR, lambda d: spread(0, d).wait_send())
     spread_start(1)
     spread_end(0)
-    for way in range(2):
-        part(1, way, 0)
-        for j in range(SUB):
-            hop(way, 0, j).start()
-    parts(1, 1)
-
-    @pl.when(r != 1)
+
+    def left_late():
+        left_a2a()
+        left_regroup()
+        left_spread()
+
+    @pl.when(r > 1)
     def _():
+        for way in range(2):
+            part(1, way, 0)
+            for j in range(SUB):
+                hop(way, 0, j).start()
+        parts(1, 1)
+        left_late()
+        ring(0)
+        ring(1)
         to_owner().start()
+        loop(2, NZ - 2, ring)
+        ring(NZ - 2)
+        out_ref[...] = rhs[...] - acc[z]
+        to_owner().wait_send()
+        drain(NZ - 2)
+
+    def no_ring():
+        spread_end(1)
+        first_in_step(2)
+        first_in_step(3)
+        left_late()
+
+    @pl.when(r == 0)
+    def _():
+        no_ring()
+        to_owner().start()
+        for k in range(NR):
+            out_ref[:, k * KB : (k + 1) * KB] = xs[1, k]
+        to_owner().wait_send()
 
     @pl.when(r == 1)
     def _():
+        no_ring()
         s1t[:, 1] = py[...]
-
-
-    for s in range(2):
-        ring(s)
-    loop(2, NZ - 2, ring)
-    ring(NZ - 2)
-
-    @pl.when(r == 0)
-    def _():
-        for k in range(NR):
-            out_ref[:, k * KB : (k + 1) * KB] = xs[1, k]
-
-    @pl.when(r == 1)
-    def _():
         loop(1, NR, lambda d: from_peer(d).wait_recv())
         for k in range(NR):
             block = s1t[k // 2, k % 2 * 8 : k % 2 * 8 + 8].reshape(KB, KB)
             out_ref[:, k * KB : (k + 1) * KB] = block.T[0:MB]
 
-    @pl.when(r > 1)
-    def _():
-        out_ref[...] = rhs[...] - acc[z]
-
-    @pl.when(r != 1)
-    def _():
-        to_owner().wait_send()
-
     left_scatter()
-    left_swap()
-    for q in range(3):
-        left_f(q)
-        left_ag(q)
-    left_a2a()
-    left_regroup()
-    left_spread()
-    left_ring()
 
 
 def local(right_side, factor):

time: 111 us -> 105 us (0.946)
  the two profiles are of different devices: /device:TPU:8 before, /device:TPU:24 now
where the time goes in v4:
time: 105 us
  Pallas kernels  103 us (98%)
  local copies, waits for them, and re-layouts  1.77 us (2%)
    pallas_call x1, Pallas kernels, local(): pl.pallas_call(kernel, name='panels', out_shape=jax.ShapeDtypeStruct((MB,...  103 us

profile of v4, /device:TPU:24, one launch (start us, length us, event | category | flops | bytes accessed | tf_op | source)
XLA Modules:
  0.0 105.0 jit_solution(3927841480243390649)
XLA Ops:
  0.0 103.2 %panels.1 = f32[48,2048]{1,0:T(8,128)} custom-call(f32[48,2048]{1,0:T(8,128)} %rhs_hbm.1, f32[4096,128]{1,0:T(8,128)} %bitcast.1), custom_call_target="tpu_custom_call" | custom-call | tf_op jit(solution)/shard_map/panels/pallas_call | solution.py:588
  103.2 1.8 %copy.4 = f32[48,2048]{1,0:T(8,128)} copy(f32[48,2048]{1,0:T(8,128)} %panels.1) | data formatting | bytes 786432

commit v5 on v4

--- a/solution.py
+++ b/solution.py
@@ -56,7 +56,7 @@
     mate = (r, c + 1 - 2 * core)
 
     def rowpeer(d):
-        return (r + d) % NR
+        return (r + d * (7 + 2 * core)) % NR
 
     def zpeer(d):
         return (z + d) % NZ
@@ -500,8 +500,7 @@
             part(q, way, s)
 
     def pass_on(way, s, j):
-        @pl.when(jnp.int32(s) < NZ - 1)
-        def _():
+        if not (isinstance(s, int) and s == NZ - 1):
             hop(way, s, j).start()
 
     def ring(s):

time: 105 us -> 104 us (level)
    pallas_call x1, Pallas kernels: 103 us -> 102 us  [local(): pl.pallas_call(kernel, name='panels', out_shape=jax.ShapeDtypeStruct((MB,...]
where the time goes in v5:
time: 104 us
  Pallas kernels  102 us (98%)
  local copies, waits for them, and re-layouts  1.77 us (2%)
    pallas_call x1, Pallas kernels, local(): pl.pallas_call(kernel, name='panels', out_shape=jax.ShapeDtypeStruct((MB,...  102 us

profile of v5, /device:TPU:24, one launch (start us, length us, event | category | flops | bytes accessed | tf_op | source)
XLA Modules:
  0.0 103.5 jit_solution(15652350006653261896)
XLA Ops:
  0.0 101.8 %panels.1 = f32[48,2048]{1,0:T(8,128)} custom-call(f32[48,2048]{1,0:T(8,128)} %rhs_hbm.1, f32[4096,128]{1,0:T(8,128)} %bitcast.1), custom_call_target="tpu_custom_call" | custom-call | tf_op jit(solution)/shard_map/panels/pallas_call | solution.py:587
  101.8 1.8 %copy.4 = f32[48,2048]{1,0:T(8,128)} copy(f32[48,2048]{1,0:T(8,128)} %panels.1) | data formatting | bytes 786432

commit v6 on v5

--- a/solution.py
+++ b/solution.py
@@ -56,7 +56,7 @@
     mate = (r, c + 1 - 2 * core)
 
     def rowpeer(d):
-        return (r + d * (7 + 2 * core)) % NR
+        return (r + d * (3 + 10 * core)) % NR
 
     def zpeer(d):
         return (z + d) % NZ
@@ -418,8 +418,6 @@
     hand_on(2, 0)
     hand_on(2, 1)
     arrive(1, (3, NZ - 3, 4))
-    swap_in()
-    convert(other, 1 - core)
     near(2)
     arrive(2, (3, NZ - 3, 4))
     ag_wait(1)
@@ -430,6 +428,8 @@
     ag_start(2)
     loop(1, NZ, lambda d: a2a(d).start())
     t[z] = xs[1, pl.ds(2 * z, 2)]
+    swap_in()
+    convert(other, 1 - core)
     left_swap()
     for q in range(2):
         left_f(q)

time: 104 us -> 104 us (level)
  no operation moved by 1% of the time
where the time goes in v6:
time: 104 us
  Pallas kernels  102 us (98%)
  local copies, waits for them, and re-layouts  1.77 us (2%)
    pallas_call x1, Pallas kernels, local(): pl.pallas_call(kernel, name='panels', out_shape=jax.ShapeDtypeStruct((MB,...  102 us

profile of v6, /device:TPU:24, one launch (start us, length us, event | category | flops | bytes accessed | tf_op | source)
XLA Modules:
  0.0 103.6 jit_solution(15359049715270457392)
XLA Ops:
  0.0 101.8 %panels.1 = f32[48,2048]{1,0:T(8,128)} custom-call(f32[48,2048]{1,0:T(8,128)} %rhs_hbm.1, f32[4096,128]{1,0:T(8,128)} %bitcast.1), custom_call_target="tpu_custom_call" | custom-call | tf_op jit(solution)/shard_map/panels/pallas_call | solution.py:587
  101.8 1.8 %copy.4 = f32[48,2048]{1,0:T(8,128)} copy(f32[48,2048]{1,0:T(8,128)} %panels.1) | data formatting | bytes 786432

commit v7 on v6

--- a/solution.py
+++ b/solution.py
@@ -517,14 +517,12 @@
                 drain(s - 1)
             if isinstance(s, int) and s == 6:
                 continue
-            if j == 0:
-                if isinstance(s, int) and s < 2:
-                    first_in_step(s + 2)
-                parts(0, s + 2)
-            if j == SUB - 1:
-                if isinstance(s, int) and s == 0:
-                    continue
-                parts(1, s + 2)
+            if j == 0 and isinstance(s, int) and s < 2:
+                first_in_step(s + 2)
+            if j < 2:
+                part(0, j, s + 2)
+            elif not (isinstance(s, int) and s == 0):
+                part(1, j - 2, s + 2)
 
     for s in range(2):
         first_in_step(s)

time: 104 us -> 104 us (level)
  no operation moved by 1% of the time
where the time goes in v7:
time: 104 us
  Pallas kernels  102 us (98%)
  local copies, waits for them, and re-layouts  1.77 us (2%)
    pallas_call x1, Pallas kernels, local(): pl.pallas_call(kernel, name='panels', out_shape=jax.ShapeDtypeStruct((MB,...  102 us

profile of v7, /device:TPU:24, one launch (start us, length us, event | category | flops | bytes accessed | tf_op | source)
XLA Modules:
  0.0 104.0 jit_solution(504950393840469344)
XLA Ops:
  0.0 102.2 %panels.1 = f32[48,2048]{1,0:T(8,128)} custom-call(f32[48,2048]{1,0:T(8,128)} %rhs_hbm.1, f32[4096,128]{1,0:T(8,128)} %bitcast.1), custom_call_target="tpu_custom_call" | custom-call | tf_op jit(solution)/shard_map/panels/pallas_call | solution.py:585
  102.2 1.8 %copy.4 = f32[48,2048]{1,0:T(8,128)} copy(f32[48,2048]{1,0:T(8,128)} %panels.1) | data formatting | bytes 786432
